TPU v7x, 32 devices: a whole 2x2x4 slice. The times are simulated.
32 devices in a mesh: wide: 16 (over z, x, core), narrow: 2 (over y).
Axes of the slice: x: 2, y: 2, z: 4, core: 2. Of those that a mesh axis runs over, the one named last changes fastest.
Arguments:
- tokens: bfloat16 [2048, 2048], P('wide'), may hold values from -6 to 6
- request_lengths: int32 [16, 3], replicated, may hold values from 1 to 64, 128 in all within a row
- w_qkv: bfloat16 [2048, 3, 2048], P(None, None, 'narrow'), may hold values from -0.19921875 to 0.19921875
- qk_gain: float32 [2, 2048], P(None, 'narrow'), may hold values from 0.5 to 7
- w_out: bfloat16 [2048, 2048], P('narrow'), may hold values from -0.125 to 0.125
- norm_gains: float32 [3, 2048], replicated, may hold values from 0.25 to 1.75
- w_router: bfloat16 [2048, 32], replicated, may hold values from -0.0625 to 0.0625
- routes: int32 [2048, 8], P('wide'), may hold values from 0 to 31, all different within a row; in each aligned block of 128 rows (0 to 127, 128 to 255, ...) at most 40 rows name the same one
- w_gate: bfloat16 [32, 2048, 1024], P('wide', None, 'narrow'), may hold values from -0.125 to 0.125
- w_up: bfloat16 [32, 2048, 1024], P('wide', None, 'narrow'), may hold values from -0.125 to 0.125
- w_down: bfloat16 [32, 1024, 2048], P('wide', 'narrow'), may hold values from -0.1875 to 0.1875
- w_proj: bfloat16 [2048, 128], replicated, may hold values from -0.125 to 0.125
- doc_vectors: bfloat16 [32768, 128], P(('wide', 'narrow')), may hold values from -6 to 6
- doc_segment: int32 [32, 1024], P(('wide', 'narrow')), may hold values from 0 to 15, never falling along the last dimension, each value on 1 to 128 neighbouring positions
- doc_request: int32 [32, 16], P(('wide', 'narrow')), may hold values from 0 to 47
Outputs:
- layer_out: bfloat16 [2048, 2048], P('wide')
- doc_scores: float32 [32, 16], P(('wide', 'narrow'))
Inputs may be any that keep to these rules, and one draw needn't show every extreme that they name: `request_lengths`: each row sums to 128, and its largest entry is exactly 64. `routes`: each row names 8 different experts. In the rows of one index of wide (aligned blocks of 128 rows) no expert is named by more than 40 rows, a bound that some block reaches. `doc_segment`: in each row the numbers never fall, every document has one or more rows, and one document has exactly 128.
All inputs are finite; a program needn't handle non-finite values.
Results may differ from a plain program's by a relative error of at most 0.009.
Values may be sent and summed in bfloat16 or wider, within the bound.
A program may use at most 128 MiB of HBM per device.

v0:
```python
import jax
import jax.numpy as jnp
from jax import lax
from jax.sharding import PartitionSpec as P

HD = 128
TOPK = 8
TOK_DEV = 128


EPS = 1e-06
THETA = 50000.0
NEG = -1e30


def rms_norm(values, gain):
    return values * lax.rsqrt(jnp.mean(values * values, axis=-1, keepdims=True) + EPS) * gain


def rotary(values, offsets):
    half = values.shape[-1] // 2
    freq = THETA ** (-jnp.arange(half, dtype=jnp.float32) / half)
    angle = offsets.astype(jnp.float32)[:, None] * freq[None, :]
    cosine = jnp.cos(angle)[:, None, :]
    sine = jnp.sin(angle)[:, None, :]
    first = values[..., :half]
    second = values[..., half:]
    return jnp.concatenate(
        [first * cosine - second * sine, second * cosine + first * sine], axis=-1
    )


def request_layout(lengths_row, count):
    bounds = jnp.cumsum(lengths_row)
    places = jnp.arange(count, dtype=jnp.int32)
    member = jnp.sum((places[:, None] >= bounds[None, :-1]).astype(jnp.int32), axis=1)
    starts = bounds - lengths_row
    pick = member[:, None] == jnp.arange(lengths_row.shape[0], dtype=jnp.int32)[None, :]
    offsets = places - jnp.sum(jnp.where(pick, starts[None, :], 0), axis=1)
    return (member, offsets)


def request_of(index, request_lengths):
    shard_count, per_shard = request_lengths.shape
    bounds = jnp.cumsum(request_lengths, axis=1)
    shard = index // TOK_DEV
    place = index - shard * TOK_DEV
    pick = shard[:, None] == jnp.arange(shard_count, dtype=jnp.int32)[None, :]
    row_bounds = jnp.sum(jnp.where(pick[:, :, None], bounds[None, :, :], 0), axis=1)
    member = jnp.sum((place[:, None] >= row_bounds[:, :-1]).astype(jnp.int32), axis=1)
    return shard * per_shard + member


def body(
    tokens,
    request_lengths,
    w_qkv,
    qk_gain,
    w_out,
    norm_gains,
    w_router,
    routes,
    w_gate,
    w_up,
    w_down,
    w_proj,
    doc_vectors,
    doc_segment,
    doc_request,
):
    f32 = jnp.float32
    bf16 = jnp.bfloat16
    count, width = tokens.shape
    experts = w_router.shape[1]
    capacity = max(2, 5 * TOK_DEV * TOPK // (4 * experts))
    heads_here = w_qkv.shape[2] // HD
    lengths_row = lax.dynamic_slice_in_dim(request_lengths, lax.axis_index("wide"), 1, 0)[0]
    member, offsets = request_layout(lengths_row, count)
    xf = tokens.astype(f32)
    normed = rms_norm(xf, norm_gains[0]).astype(bf16)
    proj = jnp.dot(normed, w_qkv.reshape(width, -1), preferred_element_type=f32).reshape(
        count, 3, heads_here, HD
    )
    query = rotary(rms_norm(proj[:, 0], qk_gain[0].reshape(heads_here, HD)), offsets).astype(bf16)
    keys = rotary(rms_norm(proj[:, 1], qk_gain[1].reshape(heads_here, HD)), offsets).astype(bf16)
    values = proj[:, 2].astype(bf16)
    scores = jnp.einsum("qhd,khd->hqk", query, keys, preferred_element_type=f32) * HD ** (-0.5)
    scores = jnp.where((member[:, None] == member[None, :])[None], scores, NEG)
    peak = jnp.max(scores, axis=-1, keepdims=True)
    weights = jnp.exp(scores - peak)
    probs = (weights / jnp.sum(weights, axis=-1, keepdims=True)).astype(bf16)
    mixed = (
        jnp.einsum("hqk,khd->qhd", probs, values, preferred_element_type=f32)
        .astype(bf16)
        .reshape(count, heads_here * HD)
    )
    attn = lax.psum(jnp.dot(mixed, w_out, preferred_element_type=f32), "narrow")
    hidden = (xf + attn).astype(bf16)
    normed_two = rms_norm(hidden.astype(f32), norm_gains[1]).astype(bf16)
    logits = jnp.dot(normed_two, w_router, preferred_element_type=f32)
    onehot = routes[:, :, None] == jnp.arange(experts, dtype=jnp.int32)[None, None, :]
    chosen = jnp.sum(jnp.where(onehot, logits[:, None, :], 0.0), axis=-1)
    lifted = jax.nn.sigmoid(chosen)
    gates = lifted / jnp.sum(lifted, axis=-1, keepdims=True)
    counts = jnp.sum(onehot.astype(bf16), axis=1)
    positions = jnp.arange(count, dtype=jnp.int32)
    lower = (positions[:, None] > positions[None, :]).astype(bf16)
    before = jnp.dot(lower, counts, preferred_element_type=f32)
    slots = jnp.sum(jnp.where(onehot, before[:, None, :], 0.0), axis=-1).astype(jnp.int32)
    places = routes * capacity + slots
    owner = (
        jnp.full((experts * capacity,), count, jnp.int32)
        .at[places.reshape(-1)]
        .set(jnp.repeat(positions, TOPK))
    )
    padded = jnp.concatenate([normed_two, jnp.zeros((1, width), bf16)], axis=0)
    buffer = padded[owner].reshape(experts, 1, capacity, width)
    received = lax.all_to_all(buffer, "wide", split_axis=0, concat_axis=1, tiled=True)
    gate = jnp.einsum("esrd,edf->esrf", received, w_gate, preferred_element_type=f32)
    upward = jnp.einsum("esrd,edf->esrf", received, w_up, preferred_element_type=f32)
    active = (jax.nn.silu(gate) * upward).astype(bf16)
    partial_out = jnp.einsum("esrf,efd->esrd", active, w_down, preferred_element_type=f32).astype(
        bf16
    )
    expert_rows = lax.all_to_all(partial_out, "wide", split_axis=1, concat_axis=0, tiled=True)
    flat_rows = expert_rows.reshape(experts * capacity, expert_rows.shape[3])
    picked = flat_rows[places]
    mixture = jnp.sum(gates[:, :, None] * picked.astype(f32), axis=1)
    moe = lax.psum(mixture.astype(jnp.bfloat16), "narrow").astype(jnp.float32)
    layer_out = (hidden.astype(f32) + moe).astype(bf16)
    normed_three = rms_norm(layer_out.astype(f32), norm_gains[2]).astype(bf16)
    embedded = jnp.dot(normed_three, w_proj, preferred_element_type=f32)
    vectors = (
        embedded * lax.rsqrt(jnp.sum(embedded * embedded, axis=-1, keepdims=True) + EPS)
    ).astype(bf16)
    segment_row = doc_segment[0]
    requests = doc_request[0]
    docs_held = requests.shape[0]
    piece = lax.all_gather(vectors, "wide", axis=0, tiled=True)
    sims = lax.dot_general(piece, doc_vectors, (((1,), (1,)), ((), ())), preferred_element_type=f32)
    owners = request_of(jnp.arange(piece.shape[0], dtype=jnp.int32), request_lengths)
    best = jnp.stack(
        [
            jnp.max(jnp.where(segment_row[None, :] == doc, sims, NEG), axis=1)
            for doc in range(docs_held)
        ],
        axis=1,
    )
    totals = jnp.sum(jnp.where(owners[:, None] == requests[None, :], best, 0.0), axis=0)
    flat_lengths = request_lengths.reshape(-1)
    request_total = flat_lengths.shape[0]
    match = requests[:, None] == jnp.arange(request_total, dtype=jnp.int32)[None, :]
    doc_lengths = jnp.sum(jnp.where(match, flat_lengths[None, :], 0), axis=1).astype(f32)
    doc_scores = (totals / doc_lengths)[None, :]
    return (layer_out, doc_scores)


def solution(mesh):
    placed = (
        P("wide", None),
        P(),
        P(None, None, "narrow"),
        P(None, "narrow"),
        P("narrow", None),
        P(),
        P(),
        P("wide", None),
        P("wide", None, "narrow"),
        P("wide", None, "narrow"),
        P("wide", "narrow", None),
        P(),
        P(("wide", "narrow"), None),
        P(("wide", "narrow"), None),
        P(("wide", "narrow"), None),
    )
    return jax.shard_map(
        body,
        mesh=mesh,
        in_specs=placed,
        out_specs=(P("wide", None), P(("wide", "narrow"), None)),
        check_vma=False,
    )
```

profile of v0, /device:TPU:0, one launch (start us, length us, event | category | flops | bytes accessed | tf_op | source)
XLA Modules:
  0.0 460.6 jit_solution(8689558873696506503)
XLA Ops:
  7.2 0.8 copy.56
  8.1 0.2 reduce-window.4
  8.3 17.0 %copy.55 = bf16[2048,3,1024]{0,2,1:T(8,128)(2,1)} copy(bf16[2048,3,1024]{2,0,1:T(8,128)(2,1)} %param.17) | data formatting | bytes 25165824 | tf_op args[2]
  25.3 0.2 fusion.30
  25.6 6.6 %fusion.39 = f32[128,3,8,128]{0,3,2,1:T(8,128)S(1)} fusion(bf16[3,8,128,2048]{3,2,1,0:T(8,128)(2,1)} %bitcast.116, bf16[128,2048]{1,0:T(8,128)(2,1)S(1)} %copy-done.2, f32[2048]{0:T(1024)S(1)} %bitcast.122, f32[128]{0:T(128)S(1)} %add_rsqrt_fusion.5), kind=kOutput, calls=%fused_computation.60 | convolution fusion | flops 1611661312 | bytes 14688768 | tf_op jit(solution)/shard_map/dot_general | solution.py:81
  32.1 0.1 multiply_reduce_fusion
  32.2 0.1 fusion.77
  32.3 0.1 broadcast_compare_fusion
  32.5 0.2 multiply_cosine_fusion
  32.7 0.3 multiply_multiply_fusion
  33.1 0.2 subtract_convert_fusion
  33.2 0.4 fusion.104
  33.6 0.5 convolution_convert_fusion
  34.2 4.0 fusion.109
  38.2 0.1 reshape.321
  38.3 0.1 fusion.58
  38.5 42.6 %all-reduce.4.cloned.1.call-done = f32[128,2048]{1,0:T(8,128)} async-done(((f32[128,2048]{1,0:T(8,128)}), f32[128,2048]{1,0:T(8,128)}) %all-reduce.4.cloned.1.call-update) | async-done | bytes 1048592 | tf_op jit(solution)/shard_map/psum | solution.py:97
  81.1 1.5 fusion.34
  82.6 0.2 fusion.36
  82.8 0.3 fusion.110
  83.2 0.1 copy.61
  83.3 0.1 reshape.297
  83.4 4.3 scatter_custom_fusion
  87.8 6.1 %gather_fusion = bf16[1280,2048]{1,0:T(8,128)(2,1)} fusion(bf16[129,2048]{1,0:T(8,128)(2,1)S(1)} %concatenate.13, s32[2048]{0:T(1024)S(1)} %pad_clamp_fusion), kind=kCustom, calls=%fused_computation | custom fusion | bytes 10490880 | tf_op jit(solution)/shard_map/gather | solution.py:117
  93.9 120.6 %all_to_all.33 = bf16[32,1,40,2048]{3,2,1,0:T(8,128)(2,1)S(1)} all-to-all(bf16[32,1,40,2048]{3,2,1,0:T(8,128)(2,1)} %bitcast.117), channel_id=1, replica_groups=mesh['wide'=16,'narrow'=2] {'wide'}, dimensions={0} | all-to-all | bytes 10485760 | tf_op jit(solution)/shard_map/all_to_all | solution.py:118
  214.5 2.3 copy-done.1
  216.8 4.4 fusion.4
  221.3 13.8 %fusion.12 = bf16[2,16,40,2048]{3,2,1,0:T(8,128)(2,1)} fusion(bf16[2,512,2048]{2,1,0:T(8,128)(2,1)} %param.25, f32[2,16,40,512]{3,2,1,0:T(8,128)} %fusion.4, bf16[2,2048,512]{2,1,0:T(8,128)(2,1)} %param.24, bf16[16,2,1,40,2048]{4,3,1,0,2:T(8,128)(2,1)} %bitcast.119), kind=kOutput, calls=%fused_computation.32 | convolution fusion | flops 5375262720 | bytes 21495808 | tf_op jit(solution)/shard_map/esrf,efd->esrd/dot_general | solution.py:122
  235.0 5.7 %copy.64 = bf16[2,16,40,2048]{3,2,0,1:T(8,128)(2,1)} copy(bf16[2,16,40,2048]{3,2,1,0:T(8,128)(2,1)} %fusion.12) | data formatting | bytes 10485760 | tf_op jit(solution)/shard_map/convert_element_type | solution.py:122
  240.7 5.6 %all-to-all-start.1 = ((bf16[2,16,40,2048]{3,2,0,1:T(8,128)(2,1)}), bf16[2,16,40,2048]{3,2,0,1:T(8,128)(2,1)}, u32[]{:S(2)}, u32[]{:S(2)}) async-start(bf16[2,16,40,2048]{3,2,0,1:T(8,128)(2,1)} %copy.64), calls=%async_computation.1 | async-start | bytes 10485760 | tf_op jit(solution)/shard_map/all_to_all | solution.py:125
  246.3 0.3 all-reduce.6.cloned.1.call-start
  246.7 0.2 select_reduce_fusion.20
  246.9 0.1 select_reduce_fusion.16
  247.1 0.1 copy.65
  247.2 0.1 reshape.311
  247.3 0.1 copy.60
  247.4 94.8 %all-to-all-done.1 = bf16[2,16,40,2048]{3,2,0,1:T(8,128)(2,1)} async-done(((bf16[2,16,40,2048]{3,2,0,1:T(8,128)(2,1)}), bf16[2,16,40,2048]{3,2,0,1:T(8,128)(2,1)}, u32[]{:S(2)}, u32[]{:S(2)}) %all-to-all-start.1) | async-done | bytes 5242912 | tf_op jit(solution)/shard_map/all_to_all | solution.py:125
  342.2 12.0 %gather_fusion.1 = bf16[1024,2048]{1,0:T(8,128)(2,1)} fusion(bf16[1280,2048]{1,0:T(8,128)(2,1)} %bitcast.33, s32[1024]{0:T(1024)S(1)} %broadcast_clamp_fusion), kind=kCustom, calls=%fused_computation.1 | custom fusion | bytes 8392704 | tf_op jit(solution)/shard_map/gather | solution.py:127
  354.3 7.4 %fusion.1 = bf16[128,2048]{1,0:T(8,128)(2,1)} fusion(bf16[1024,2048]{1,0:T(8,128)(2,1)} %gather_fusion.1, f32[128,8]{1,0:T(8,128)S(1)} %copy.60), kind=kLoop, calls=%fused_computation.5 | loop fusion | flops 6029312 | bytes 4722688 | tf_op jit(solution)/shard_map/reduce_sum | solution.py:128
  361.7 0.2 compare_reduce_fusion
  361.9 46.7 %all-reduce.6.cloned.1.call-done = bf16[128,2048]{1,0:T(8,128)(2,1)} async-done(((bf16[128,2048]{1,0:T(8,128)(2,1)}), bf16[128,2048]{1,0:T(8,128)(2,1)}) %all-reduce.6.cloned.1.call-update) | async-done | bytes 524304 | tf_op jit(solution)/shard_map/psum | solution.py:129
  408.6 1.3 fusion.27
  410.0 0.4 multiply_reduce_fusion.2
  410.4 22.9 %all_gather.3 = bf16[2048,128]{0,1:T(8,128)(2,1)S(1)} all-gather(bf16[128,128]{0,1:T(8,128)(2,1)S(1)} %multiply_convert_fusion.1), channel_id=1, replica_groups=mesh['wide'=16,'narrow'=2] {'wide'}, dimensions={0}, use_global_device_ids=true | all-gather | bytes 557056 | tf_op jit(solution)/shard_map/all_gather | solution.py:139
  433.3 19.5 %select_reduce_fusion = (f32[2048]{0:T(1024)S(1)}, f32[2048]{0:T(1024)S(1)}, f32[2048]{0:T(1024)S(1)}, f32[2048]{0:T(1024)S(1)}, f32[2048]{0:T(1024)S(1)}, /*ind...) fusion(pred[1024]{0:T(1024)(128)(4,1)S(1)} %get-tuple-element.2, ...), kind=kOutput, calls=%fused_computation.6 | convolution fusion | flops 603947008 | bytes 933888 | tf_op jit(solution)/shard_map/dot_general | solution.py:140
  452.8 0.2 stack.67
  453.0 0.2 select_reduce_fusion.17
  453.2 0.5 fusion.79
  (60 shorter events, 0.7 us)
Async XLA Ops:
  7.2 402.8 %copy-start = (bf16[2048,128]{1,0:T(8,128)(2,1)S(1)}, bf16[2048,128]{1,0:T(8,128)(2,1)}, u32[]{:S(2)}) copy-start(bf16[2048,128]{1,0:T(8,128)(2,1)} %param.26) | copy-start | bytes 1572868
  7.2 73.9 %all-reduce.4.cloned.1.call-start = ((), (), s32[]{:S(2)}) async-start(), calls=%async_computation.2 | async-start | bytes 2097152 | tf_op jit(solution)/shard_map/psum | solution.py:97
  8.2 17.1 %copy-start.6 = (f32[3,2048]{1,0:T(4,128)S(1)}, f32[3,2048]{1,0:T(4,128)}, u32[]{:S(2)}) copy-start(f32[3,2048]{1,0:T(4,128)} %param.20) | copy-start | bytes 73732
  8.3 17.1 %copy-start.2 = (bf16[128,2048]{1,0:T(8,128)(2,1)S(1)}, bf16[128,2048]{1,0:T(8,128)(2,1)}, u32[]{:S(2)}) copy-start(bf16[128,2048]{1,0:T(8,128)(2,1)} %param.15) | copy-start | bytes 1572868
  8.3 17.3 %copy-start.8 = (f32[2,1024]{1,0:T(2,128)S(1)}, f32[2,1024]{1,0:T(2,128)}, u32[]{:S(2)}) copy-start(f32[2,1024]{1,0:T(2,128)} %param.18) | copy-start | bytes 24580
  34.1 4.2 copy-start.5
  34.2 48.7 %copy-start.4 = (bf16[2048,32]{0,1:T(8,128)(2,1)S(1)}, bf16[2048,32]{0,1:T(8,128)(2,1)}, u32[]{:S(2)}) copy-start(bf16[2048,32]{0,1:T(8,128)(2,1)} %param.21) | copy-start | bytes 393220
  93.9 123.0 %copy-start.11 = (bf16[2,2048,512]{2,1,0:T(8,128)(2,1)S(1)}, bf16[2,2048,512]{2,1,0:T(8,128)(2,1)}, u32[]{:S(2)}) copy-start(bf16[2,2048,512]{2,1,0:T(8,128)(2,1)} %param.23) | copy-start | bytes 12582916
  214.5 2.3 copy-start.1
  240.7 5.8 %copy-start.7 = (s32[16,3]{0,1:T(4,128)S(1)}, s32[16,3]{0,1:T(4,128)}, u32[]{:S(2)}) copy-start(s32[16,3]{0,1:T(4,128)} %param.16) | copy-start | bytes 580
  240.7 6.0 %copy-start.10 = (s32[1,16]{1,0:T(1,128)S(1)}, s32[1,16]{1,0:T(1,128)}, u32[]{:S(2)}) copy-start(s32[1,16]{1,0:T(1,128)} %param.29) | copy-start | bytes 196
  240.7 101.5 %all-to-all-start.1 = ((bf16[2,16,40,2048]{3,2,0,1:T(8,128)(2,1)}), bf16[2,16,40,2048]{3,2,0,1:T(8,128)(2,1)}, u32[]{:S(2)}, u32[]{:S(2)}) async-start(bf16[2,16,40,2048]{3,2,0,1:T(8,128)(2,1)} %copy.64), calls=%async_computation.1 | async-start | bytes 10485760 | tf_op jit(solution)/shard_map/all_to_all | solution.py:125
  246.3 162.4 %all-reduce.6.cloned.1.call-start = ((), (), s32[]{:S(2)}) async-start(), calls=%async_computation.3 | async-start | bytes 1048576 | tf_op jit(solution)/shard_map/psum | solution.py:129
  354.3 7.4 %copy-start.9 = (s32[1,1024]{1,0:T(1,128)S(1)}, s32[1,1024]{1,0:T(1,128)}, u32[]{:S(2)}) copy-start(s32[1,1024]{1,0:T(1,128)} %param.28) | copy-start | bytes 12292
  354.3 79.0 %copy-start.12 = (bf16[1024,128]{1,0:T(8,128)(2,1)S(1)}, bf16[1024,128]{1,0:T(8,128)(2,1)}, u32[]{:S(2)}) copy-start(bf16[1024,128]{1,0:T(8,128)(2,1)} %param.27) | copy-start | bytes 786436
  410.0 42.8 %copy-start.3 = (bf16[128,2048]{1,0:T(8,128)(2,1)}, bf16[128,2048]{1,0:T(8,128)(2,1)S(1)}, u32[]{:S(2)}) copy-start(bf16[128,2048]{1,0:T(8,128)(2,1)S(1)} %get-tuple-element.39) | copy-start | bytes 1572868
Sparse Core Ops, SparseCore 0:
  38.3 42.7 all-reduce.3
  361.8 46.8 all-reduce.5
where the time goes:
time: 461 us
  waiting for transfers between devices  184 us (40%)
  blocking collectives  143 us (31%)
  matrix products  50 us (11%)
  local copies, waits for them, and re-layouts  49.4 us (11%)
  between operations  14.4 us (3%)
  other arithmetic  13.3 us (3%)
  starting transfers between devices  5.85 us (1%)
    all_to_all x1, blocking collectives, body(): lax.all_to_all(buffer, 'wide', split_axis=0, concat_axis=1, tiled=True)  121 us
    all_to_all x1, waiting for transfers between devices, body(): lax.all_to_all(partial_out, 'wide', split_axis=1, concat_axis=0, tiled=True)  94.8 us
    psum x1, waiting for transfers between devices, body(): moe = lax.psum(mixture.astype(jnp.bfloat16), 'narrow').astype(jnp.float32)  46.7 us
    psum x1, waiting for transfers between devices, body(): attn = lax.psum(jnp.dot(mixed, w_out, preferred_element_type=f32), 'narrow')  42.6 us
    all_gather x1, blocking collectives, body(): piece = lax.all_gather(vectors, 'wide', axis=0, tiled=True)  22.9 us
    unnamed x28, local copies, waits for them, and re-layouts  20.2 us
    dot_general x1, matrix products, body(): lax.dot_general(piece, doc_vectors, (((1,), (1,)), ((), ())), preferred_e...  19.5 us
    dot_general x1, matrix products, body(): jnp.einsum('esrf,efd->esrd', active, w_down, preferred_element_type=f32)  13.8 us
  transfers between devices with their start and end apart: 3, of which 3 were waited for; matrix products, arithmetic and copies ran while one was open for 0% of the time, Pallas kernels for 0%

commit v1 on v0

v1 whole, which is shorter than its diff:
```python
import functools

import jax
import jax.numpy as jnp
from jax import lax
from jax.experimental import pallas as pl
from jax.experimental.pallas import tpu as pltpu
from jax.sharding import PartitionSpec as P

HD = 128
TOK_DEV = 128
MOST_REQ = 64
DOC_MOST = 128
LANES = 128

EPS = 1e-06
THETA = 50000.0
NEG = -1e30
MIB = 1 << 20

f32 = jnp.float32
bf16 = jnp.bfloat16
VMEM = pl.BlockSpec(memory_space=pltpu.VMEM)


def rms_norm(values, gain):
    return values * lax.rsqrt(jnp.mean(values * values, axis=-1, keepdims=True) + EPS) * gain


def request_layout(lengths_row, count):
    bounds = jnp.cumsum(lengths_row)
    places = jnp.arange(count, dtype=jnp.int32)
    member = jnp.sum((places[:, None] >= bounds[None, :-1]).astype(jnp.int32), axis=1)
    starts = bounds - lengths_row
    pick = member[:, None] == jnp.arange(lengths_row.shape[0], dtype=jnp.int32)[None, :]
    offsets = places - jnp.sum(jnp.where(pick, starts[None, :], 0), axis=1)
    return (member, offsets)


def front_kernel(tokens, gain, w_qkv, qk_gain, cosine, sine, bias, mixed, normed):
    @pl.when(pl.program_id(0) == 0)
    def _():
        normed[...] = rms_norm(tokens[...].astype(f32), gain[...]).astype(bf16)

    heads = mixed.shape[1] // HD
    parts = [jnp.dot(normed[...], w_qkv[i], preferred_element_type=f32) for i in range(3)]
    for head in range(heads):
        lanes = slice(head * HD, (head + 1) * HD)

        def turned(part):
            v = rms_norm(parts[part][:, lanes], qk_gain[part : part + 1, lanes])
            return (v * cosine[...] + pltpu.roll(v, HD // 2, 1) * sine[...]).astype(bf16)

        query, keys = turned(0), turned(1)
        values = parts[2][:, lanes].astype(bf16)
        scores = lax.dot_general(
            query, keys, (((1,), (1,)), ((), ())), preferred_element_type=f32
        ) * (HD ** (-0.5))
        scores = jnp.where(bias[...] > 0, scores, NEG)
        weights = jnp.exp(scores - jnp.max(scores, axis=-1, keepdims=True))
        probs = (weights / jnp.sum(weights, axis=-1, keepdims=True)).astype(bf16)
        mixed[:, lanes] = jnp.dot(probs, values, preferred_element_type=f32).astype(bf16)


def partner_barrier(other):
    barrier = pltpu.get_barrier_semaphore()
    pl.semaphore_signal(
        barrier, inc=1, device_id={"narrow": other}, device_id_type=pl.DeviceIdType.MESH
    )
    pl.semaphore_wait(barrier, 1)


def join_kernel(
    pieces, experts, mixed, w_out, tokens, gain, w_router, routes,
    hidden, extended, mine, theirs, send_sem, recv_sem,
):
    other = 1 - lax.axis_index("narrow")
    partner_barrier(other)
    width = w_out.shape[1]
    step = width // pieces
    copies = []
    for piece in range(pieces):
        lanes = pl.ds(piece * step, step)
        mine[piece] = jnp.dot(mixed[...], w_out[:, lanes], preferred_element_type=f32).astype(bf16)
        copy = pltpu.make_async_remote_copy(
            src_ref=mine.at[piece],
            dst_ref=theirs.at[piece],
            send_sem=send_sem.at[piece],
            recv_sem=recv_sem.at[piece],
            device_id={"narrow": other},
            device_id_type=pl.DeviceIdType.MESH,
        )
        copy.start()
        copies.append(copy)
    total = 0.0
    for piece in range(pieces):
        lanes = pl.ds(piece * step, step)
        copies[piece].wait()
        attn = mine[piece].astype(f32) + theirs[piece].astype(f32)
        row = (tokens[:, lanes].astype(f32) + attn).astype(bf16)
        hidden[:, lanes] = row
        row = row.astype(f32)
        total = total + jnp.sum(row * row, axis=-1, keepdims=True)
    scale = lax.rsqrt(total / width + EPS)
    normed = (hidden[...].astype(f32) * scale * gain[...]).astype(bf16)
    extended[:, :width] = normed
    logits = jnp.dot(normed, w_router[...], preferred_element_type=f32)
    lane = lax.broadcasted_iota(jnp.int32, logits.shape, 1)
    expert = jnp.where(lane < experts, lane, lane - experts)
    routed = routes[:, 0:1] == expert
    for k in range(1, routes.shape[1]):
        routed = routed | (routes[:, k : k + 1] == expert)
    lifted = jnp.where(routed, 1.0 / (1.0 + jnp.exp(-logits)), 0.0)
    first = lane < experts
    gates = lifted / jnp.sum(jnp.where(first, lifted, 0.0), axis=-1, keepdims=True)
    high = gates.astype(bf16).astype(f32)
    extended[:, width:] = jnp.where(first, high, gates - high).astype(bf16)


def moe_kernel(rows, chosen, w_gate, w_up, w_down, out):
    width = out.shape[1]
    x = rows[:, :width]
    table = rows[:, width:].astype(f32)
    total = 0.0
    for e in range(w_gate.shape[0]):
        gate = jnp.sum(table * chosen[e : e + 1, :], axis=-1, keepdims=True)
        lift = jnp.dot(x, w_gate[e], preferred_element_type=f32)
        upward = jnp.dot(x, w_up[e], preferred_element_type=f32)
        active = (lift / (1.0 + jnp.exp(-lift)) * upward * gate).astype(bf16)
        total = total + jnp.dot(active, w_down[e], preferred_element_type=f32)
    out[...] = total.astype(bf16)


def tail_kernel(
    pieces, partial_out, hidden, gain, w_proj, layer_out, vectors, theirs, send_sem, recv_sem
):
    other = 1 - lax.axis_index("narrow")
    partner_barrier(other)
    width = hidden.shape[1]
    step = hidden.shape[0] // pieces
    copies = []
    for piece in range(pieces):
        rows = pl.ds(piece * step, step)
        copy = pltpu.make_async_remote_copy(
            src_ref=partial_out.at[rows],
            dst_ref=theirs.at[rows],
            send_sem=send_sem.at[piece],
            recv_sem=recv_sem.at[piece],
            device_id={"narrow": other},
            device_id_type=pl.DeviceIdType.MESH,
        )
        copy.start()
        copies.append(copy)
    for piece in range(pieces):
        rows = pl.ds(piece * step, step)
        copies[piece].wait()
        moe = partial_out[rows, :].astype(f32) + theirs[rows, :].astype(f32)
        out = (hidden[rows, :].astype(f32) + moe).astype(bf16)
        layer_out[rows, :] = out
        normed = rms_norm(out.astype(f32), gain[...]).astype(bf16)
        embedded = jnp.dot(normed, w_proj[...], preferred_element_type=f32)
        vectors[rows, :] = (
            embedded * lax.rsqrt(jnp.sum(embedded * embedded, axis=-1, keepdims=True) + EPS)
        ).astype(bf16)


def docs_kernel(plan, vectors, docs, scores):
    held = scores.shape[1]
    q_rows = MOST_REQ + 16
    d_rows = DOC_MOST + 128
    lane = lax.broadcasted_iota(jnp.int32, (1, held), 1)
    row = lax.broadcasted_iota(jnp.int32, (q_rows, 1), 0)
    column = lax.broadcasted_iota(jnp.int32, (1, d_rows), 1)
    out = jnp.zeros((1, held), f32)
    for doc in range(held):
        q_first, q_size = plan[0, doc], plan[1, doc]
        d_first, d_size = plan[2, doc], plan[3, doc]
        q_at = pl.multiple_of(jnp.minimum(q_first // 16 * 16, vectors.shape[0] - q_rows), 16)
        d_at = pl.multiple_of(jnp.minimum(d_first // 16 * 16, docs.shape[0] - d_rows), 16)
        sims = lax.dot_general(
            vectors[pl.ds(q_at, q_rows), :],
            docs[pl.ds(d_at, d_rows), :],
            (((1,), (1,)), ((), ())),
            preferred_element_type=f32,
        )
        place = column + d_at
        sims = jnp.where((place >= d_first) & (place < d_first + d_size), sims, NEG)
        best = jnp.max(sims, axis=1, keepdims=True)
        place = row + q_at
        best = jnp.where((place >= q_first) & (place < q_first + q_size), best, 0.0)
        total = jnp.sum(best, axis=0, keepdims=True) / q_size.astype(f32)
        out = jnp.where(lane == doc, total, out)
    scores[...] = out


def body(
    tokens,
    request_lengths,
    w_qkv,
    qk_gain,
    w_out,
    norm_gains,
    w_router,
    routes,
    w_gate,
    w_up,
    w_down,
    w_proj,
    doc_vectors,
    doc_segment,
    doc_request,
):
    count, width = tokens.shape
    experts = w_router.shape[1]
    experts_here = w_gate.shape[0]
    columns = w_qkv.shape[2]
    shards = request_lengths.shape[0]
    wide = lax.axis_index("wide")
    narrow = lax.axis_index("narrow")

    lengths_row = lax.dynamic_slice_in_dim(request_lengths, wide, 1, 0)[0]
    member, offsets = request_layout(lengths_row, count)
    half = HD // 2
    freq = THETA ** (-jnp.arange(half, dtype=f32) / half)
    angle = offsets.astype(f32)[:, None] * freq[None, :]
    cosine, sine = jnp.cos(angle), jnp.sin(angle)
    cosine = jnp.concatenate([cosine, cosine], axis=1)
    sine = jnp.concatenate([-sine, sine], axis=1)
    same = (member[:, None] == member[None, :]).astype(f32)

    block = 256
    mixed = pl.pallas_call(
        front_kernel,
        out_shape=jax.ShapeDtypeStruct((count, columns), bf16),
        grid=(columns // block,),
        in_specs=[
            pl.BlockSpec((count, width), lambda i: (0, 0)),
            pl.BlockSpec((1, width), lambda i: (0, 0)),
            pl.BlockSpec((3, width, block), lambda i: (0, 0, i)),
            pl.BlockSpec((2, block), lambda i: (0, i)),
            pl.BlockSpec((count, HD), lambda i: (0, 0)),
            pl.BlockSpec((count, HD), lambda i: (0, 0)),
            pl.BlockSpec((count, count), lambda i: (0, 0)),
        ],
        out_specs=pl.BlockSpec((count, block), lambda i: (0, i)),
        scratch_shapes=[pltpu.VMEM((count, width), bf16)],
        compiler_params=pltpu.CompilerParams(vmem_limit_bytes=24 * MIB),
        name="front",
    )(tokens, norm_gains[0:1], jnp.transpose(w_qkv, (1, 0, 2)), qk_gain, cosine, sine, same)

    extra = (2 * experts + LANES - 1) // LANES * LANES
    routers = jnp.concatenate(
        [w_router, w_router, jnp.zeros((width, extra - 2 * experts), bf16)], axis=1
    )
    pieces = 4
    hidden, extended = pl.pallas_call(
        functools.partial(join_kernel, pieces, experts),
        out_shape=(
            jax.ShapeDtypeStruct((count, width), bf16),
            jax.ShapeDtypeStruct((count, width + extra), bf16),
        ),
        in_specs=[VMEM] * 6,
        out_specs=(VMEM, VMEM),
        scratch_shapes=[
            pltpu.VMEM((pieces, count, width // pieces), bf16),
            pltpu.VMEM((pieces, count, width // pieces), bf16),
            pltpu.SemaphoreType.DMA((pieces,)),
            pltpu.SemaphoreType.DMA((pieces,)),
        ],
        compiler_params=pltpu.CompilerParams(
            collective_id=0, has_side_effects=True, vmem_limit_bytes=24 * MIB
        ),
        name="join",
    )(mixed, w_out, tokens, norm_gains[1:2], routers, routes)

    share = count // lax.axis_size("narrow")
    own_rows = lax.dynamic_slice_in_dim(extended, narrow * share, share, 0)
    rows = lax.all_gather(own_rows, ("wide", "narrow"), axis=0, tiled=True)

    ids = wide * experts_here + jnp.arange(experts_here, dtype=jnp.int32)
    lane = jnp.arange(extra, dtype=jnp.int32)[None, :]
    chosen = ((lane == ids[:, None]) | (lane == ids[:, None] + experts)).astype(f32)
    every = rows.shape[0]
    block = 256
    partial_out = pl.pallas_call(
        moe_kernel,
        out_shape=jax.ShapeDtypeStruct((every, width), bf16),
        grid=(every // block,),
        in_specs=[
            pl.BlockSpec((block, width + extra), lambda i: (i, 0)),
            pl.BlockSpec(chosen.shape, lambda i: (0, 0)),
            pl.BlockSpec(w_gate.shape, lambda i: (0, 0, 0)),
            pl.BlockSpec(w_up.shape, lambda i: (0, 0, 0)),
            pl.BlockSpec(w_down.shape, lambda i: (0, 0, 0)),
        ],
        out_specs=pl.BlockSpec((block, width), lambda i: (i, 0)),
        compiler_params=pltpu.CompilerParams(vmem_limit_bytes=48 * MIB),
        name="experts",
    )(rows, chosen, w_gate, w_up, w_down)

    scattered = lax.psum_scatter(partial_out, "wide", scatter_dimension=0, tiled=True)

    pieces = 4
    layer_out, vectors = pl.pallas_call(
        functools.partial(tail_kernel, pieces),
        out_shape=(
            jax.ShapeDtypeStruct((count, width), bf16),
            jax.ShapeDtypeStruct((count, w_proj.shape[1]), bf16),
        ),
        in_specs=[VMEM] * 4,
        out_specs=(VMEM, VMEM),
        scratch_shapes=[
            pltpu.VMEM((count, width), bf16),
            pltpu.SemaphoreType.DMA((pieces,)),
            pltpu.SemaphoreType.DMA((pieces,)),
        ],
        compiler_params=pltpu.CompilerParams(
            collective_id=1, has_side_effects=True, vmem_limit_bytes=24 * MIB
        ),
        name="tail",
    )(scattered, hidden, norm_gains[2:3], w_proj)

    every_vector = lax.all_gather(vectors, "wide", axis=0, tiled=True)

    flat_lengths = request_lengths.reshape(-1)
    starts = jnp.cumsum(request_lengths, axis=1) - request_lengths
    flat_starts = (starts + TOK_DEV * jnp.arange(shards, dtype=jnp.int32)[:, None]).reshape(-1)
    requests = doc_request[0]
    pick = requests[:, None] == jnp.arange(flat_lengths.shape[0], dtype=jnp.int32)[None, :]
    docs = jnp.arange(requests.shape[0], dtype=jnp.int32)[:, None]
    plan = jnp.stack(
        [
            jnp.sum(jnp.where(pick, flat_starts[None, :], 0), axis=1),
            jnp.sum(jnp.where(pick, flat_lengths[None, :], 0), axis=1),
            jnp.sum((doc_segment < docs).astype(jnp.int32), axis=1),
            jnp.sum((doc_segment == docs).astype(jnp.int32), axis=1),
        ]
    )
    doc_scores = pl.pallas_call(
        docs_kernel,
        out_shape=jax.ShapeDtypeStruct((1, requests.shape[0]), f32),
        in_specs=[pl.BlockSpec(memory_space=pltpu.SMEM), VMEM, VMEM],
        out_specs=VMEM,
        name="docs",
    )(plan, every_vector, doc_vectors)
    return (layer_out, doc_scores)


def solution(mesh):
    placed = (
        P("wide", None),
        P(),
        P(None, None, "narrow"),
        P(None, "narrow"),
        P("narrow", None),
        P(),
        P(),
        P("wide", None),
        P("wide", None, "narrow"),
        P("wide", None, "narrow"),
        P("wide", "narrow", None),
        P(),
        P(("wide", "narrow"), None),
        P(("wide", "narrow"), None),
        P(("wide", "narrow"), None),
    )
    return jax.shard_map(
        body,
        mesh=mesh,
        in_specs=placed,
        out_specs=(P("wide", None), P(("wide", "narrow"), None)),
        check_vma=False,
    )
```

time: 461 us -> 313 us (0.68)
  blocking collectives: 143 us -> 23.1 us
  Pallas kernels: 0 us -> 74 us
  matrix products: 50 us -> 0 us
  local copies, waits for them, and re-layouts: 49.4 us -> 15.7 us
  other arithmetic: 13.3 us -> 2.22 us
  starting transfers between devices: 5.85 us -> 0.08 us
    all_to_all x1 -> x0, blocking collectives: 121 us -> none  [body(): lax.all_to_all(buffer, 'wide', split_axis=0, concat_axis=1, tiled=True)]
    reduce_scatter x0 -> x1, waiting for transfers between devices: none -> 102 us  [body(): lax.psum_scatter(partial_out, 'wide', scatter_dimension=0, tiled=True)]
    all_to_all x1 -> x0, waiting for transfers between devices: 94.8 us -> none  [body(): lax.all_to_all(partial_out, 'wide', split_axis=1, concat_axis=0, tiled=True)]
    psum x2 -> x0, waiting for transfers between devices: 89.4 us -> none  [the longest x1 46.7 us: body(): moe = lax.psum(mixture.astype(jnp.bfloat16), 'narrow').astype(jnp.float32)]
    all_gather x0 -> x1, waiting for transfers between devices: none -> 81.2 us  [body(): rows = lax.all_gather(own_rows, ('wide', 'narrow'), axis=0, tiled=True)]
    pallas_call x0 -> x5, Pallas kernels: none -> 74 us  [the longest x1 33.6 us: body(): pl.pallas_call(moe_kernel, out_shape=jax.ShapeDtypeStruct((every, width),...]
    dot_general x9 -> x0, matrix products: 49.6 us -> none  [the longest x1 19.5 us: body(): lax.dot_general(piece, doc_vectors, (((1,), (1,)), ((), ())), preferred_e...]
    gather x2 -> x0, local copies, waits for them, and re-layouts: 18.2 us -> none  [the longest x1 12 us: body(): picked = flat_rows[places]]
  transfers between devices with their start and end apart: 3 -> 2, of which waited for: 3 -> 2; matrix products, arithmetic and copies ran while one was open for 0% -> 0% of each run, Pallas kernels for 0% -> 0%
where the time goes in v1:
time: 313 us; the launch traced here: 312 us
  waiting for transfers between devices  183 us (58%)
  Pallas kernels  74 us (24%)
  blocking collectives  23.1 us (7%)
  local copies, waits for them, and re-layouts  15.7 us (5%)
  between operations  14.2 us (5%)
    reduce_scatter x1, waiting for transfers between devices, body(): lax.psum_scatter(partial_out, 'wide', scatter_dimension=0, tiled=True)  102 us
    all_gather x1, waiting for transfers between devices, body(): rows = lax.all_gather(own_rows, ('wide', 'narrow'), axis=0, tiled=True)  81.2 us
    pallas_call x1, Pallas kernels, body(): pl.pallas_call(moe_kernel, out_shape=jax.ShapeDtypeStruct((every, width),...  33.6 us
    all_gather x1, blocking collectives, body(): every_vector = lax.all_gather(vectors, 'wide', axis=0, tiled=True)  23.1 us
    pallas_call x1, Pallas kernels, body(): pl.pallas_call(functools.partial(join_kernel, pieces, experts), out_shape...  15.9 us
    pallas_call x1, Pallas kernels, body(): pl.pallas_call(functools.partial(tail_kernel, pieces), out_shape=(jax.Sha...  14.2 us
    unnamed x24, local copies, waits for them, and re-layouts  13.7 us
    pallas_call x1, Pallas kernels, body(): pl.pallas_call(front_kernel, out_shape=jax.ShapeDtypeStruct((count, colum...  7.96 us
  transfers between devices with their start and end apart: 2, of which 2 were waited for; matrix products, arithmetic and copies ran while one was open for 0% of the time, Pallas kernels for 0%

profile of v1, /device:TPU:0, one launch (start us, length us, event | category | flops | bytes accessed | tf_op | source)
XLA Modules:
  0.0 312.2 jit_solution(11513192331024254548)
XLA Ops:
  7.2 0.0 all-gather.2.cloned.1.call-start
  7.2 0.8 copy.29
  8.0 0.2 reduce-window.4
  8.2 0.1 fusion.1
  8.3 0.1 compare_convert_fusion.bias
  8.4 0.1 select_reduce_fusion.2
  8.5 0.9 fusion.4
  9.4 0.8 copy.32.routes
  10.2 1.2 copy.30
  11.3 0.1 pad.6.clone
  11.4 0.3 fusion
  11.7 0.3 maximum_maximum_fusion.w_router
  12.1 0.1 pad_maximum_fusion
  12.2 0.0 copy-start
  12.2 4.6 %copy-done = bf16[2048,3,1024]{2,0,1:T(8,128)(2,1)S(1)} copy-done((bf16[2048,3,1024]{2,0,1:T(8,128)(2,1)S(1)}, bf16[2048,3,1024]{2,0,1:T(8,128)(2,1)}, u32[]{:S(2)}) %copy-start) | copy-done | bytes 12582936
  16.8 0.0 copy-start.3
  16.8 1.0 copy-done.3
  17.8 0.0 copy-start.6
  17.8 0.7 copy-done.6
  18.5 0.0 copy-start.1
  18.5 8.0 %front.1.mixed = bf16[128,1024]{1,0:T(8,128)(2,1)S(1)} custom-call(bf16[128,2048]{1,0:T(8,128)(2,1)S(1)} %copy-done.3, f32[1,2048]{1,0:T(1,128)S(1)} %get-tuple-element.15.gain, bf16[3,2048,1024]{2,1,0:T(8,128)(2,1)S(1)} %bitcast.17, f32[2,1024]{1,0:T(2,128)S(1)} %copy-done.6, f32[128,128]{1,0:T(8,128)S(1)} %get-tuple-element.20.cosine, ...), custom_call_target="tpu_custom_call" | custom-call | tf_op jit(solution)/shard_map/front/pallas_call | solution.py:232
  26.5 0.0 copy-done.1
  26.5 15.9 %join.1 = (bf16[128,2048]{1,0:T(8,128)(2,1)S(1)}, bf16[128,2176]{1,0:T(8,128)(2,1)S(1)}) custom-call(bf16[128,1024]{1,0:T(8,128)(2,1)S(1)} %front.1.mixed, bf16[1024,2048]{1,0:T(8,128)(2,1)S(1)} %copy-done.1, bf16[128,2048]{1,0:T(8,128)(2,1)S(1)} %copy-done.3, f32[1,2048]{1,0:T(1,128)S(1)} %get-tuple-element.16.gain, ...), custom_call_target="tpu_custom_call" | custom-call | tf_op jit(solution)/shard_map/join/pallas_call | solution.py:256
  42.4 0.7 constant_dynamic-slice_fusion
  43.1 0.0 all-gather.2.cloned.1.call-update
  43.2 0.0 reduce-scatter.2.cloned.1.call-start
  43.2 0.1 or_convert_fusion.chosen
  43.3 81.2 %all-gather.2.cloned.1.call-done.rows = bf16[2048,2176]{1,0:T(8,128)(2,1)} async-done(((bf16[64,2176]{1,0:T(8,128)(2,1)}), bf16[2048,2176]{1,0:T(8,128)(2,1)}) %all-gather.2.cloned.1.call-update) | async-done | bytes 8912912 | tf_op jit(solution)/shard_map/all_gather | solution.py:278
  124.6 2.2 copy-done.2
  126.7 33.6 %experts.1 = bf16[2048,2048]{1,0:T(8,128)(2,1)} custom-call(bf16[2048,2176]{1,0:T(8,128)(2,1)} %all-gather.2.cloned.1.call-done.rows, f32[2,128]{1,0:T(2,128)S(1)} %or_convert_fusion.chosen, bf16[2,2048,512]{2,1,0:T(8,128)(2,1)S(1)} %copy-done.2, bf16[2,2048,512]{2,1,0:T(8,128)(2,1)} %w_up.1, bf16[2,512,2048]{2,1,0:T(8,128)(2,1)} %w_down.1), custom_call_target="tpu_custom_call" | custom-call | tf_op jit(solution)/shard_map/experts/pallas_call | solution.py:285
  160.4 0.0 copy-start.4
  160.4 0.0 reduce-scatter.2.cloned.1.call-update
  160.4 0.6 copy-done.7
  161.1 0.1 broadcast_in_dim.61
  161.2 0.1 copy.33
  161.3 0.1 broadcast_in_dim.58
  161.4 0.0 copy-done.9
  161.4 0.2 select_reduce_fusion.1
  161.6 0.0 copy-done.8
  161.6 0.1 convert_reduce_fusion.1
  161.7 0.6 pad_add_fusion.plan
  162.3 101.6 %reduce-scatter.2.cloned.1.call-done.partial_out = bf16[128,2048]{1,0:T(8,128)(2,1)} async-done(((bf16[2048,2048]{1,0:T(8,128)(2,1)}), bf16[128,2048]{1,0:T(8,128)(2,1)}) %reduce-scatter.2.cloned.1.call-update) | async-done | bytes 524304 | tf_op jit(solution)/shard_map/reduce_scatter | solution.py:301
  263.9 0.0 copy-done.4
  263.9 1.0 copy-done.5
  264.9 14.2 %tail.1 = (bf16[128,2048]{1,0:T(8,128)(2,1)S(1)}, bf16[128,128]{1,0:T(8,128)(2,1)S(1)}) custom-call(bf16[128,2048]{1,0:T(8,128)(2,1)S(1)} %copy-done.5, bf16[128,2048]{1,0:T(8,128)(2,1)S(1)} %get-tuple-element.7.hidden, f32[1,2048]{1,0:T(1,128)S(1)} %get-tuple-element.14.gain, bf16[2048,128]{1,0:T(8,128)(2,1)S(1)} %copy-done.4), custom_call_target="tpu_custom_call" | custom-call | tf_op jit(solution)/shard_map/tail/pallas_call | solution.py:304
  279.1 23.1 %all_gather.7.vectors = bf16[2048,128]{1,0:T(8,128)(2,1)} all-gather(bf16[128,128]{1,0:T(8,128)(2,1)S(1)} %get-tuple-element.9), channel_id=1, replica_groups=mesh['wide'=16,'narrow'=2] {'wide'}, dimensions={0}, use_global_device_ids=true | all-gather | bytes 557056 | tf_op jit(solution)/shard_map/all_gather | solution.py:323
  302.3 2.3 docs.2
  304.5 0.8 copy.36
  (15 shorter events, 0.1 us)
Async XLA Ops:
  7.2 117.4 %all-gather.2.cloned.1.call-start = ((), (), s32[]{:S(2)}) async-start(), calls=%async_computation.1 | async-start | bytes 9191424 | tf_op jit(solution)/shard_map/all_gather | solution.py:278
  12.2 4.6 %copy-start = (bf16[2048,3,1024]{2,0,1:T(8,128)(2,1)S(1)}, bf16[2048,3,1024]{2,0,1:T(8,128)(2,1)}, u32[]{:S(2)}) copy-start(bf16[2048,3,1024]{2,0,1:T(8,128)(2,1)} %param.17) | copy-start | bytes 37748740
  16.8 1.0 copy-start.3
  17.8 0.7 copy-start.6
  18.5 8.0 %copy-start.1 = (bf16[1024,2048]{1,0:T(8,128)(2,1)S(1)}, bf16[1024,2048]{1,0:T(8,128)(2,1)}, u32[]{:S(2)}) copy-start(bf16[1024,2048]{1,0:T(8,128)(2,1)} %w_out.1) | copy-start | bytes 12582916
  43.2 220.7 %reduce-scatter.2.cloned.1.call-start = ((), (), s32[]{:S(2)}) async-start(), calls=%async_computation.2 | async-start | bytes 8912896 | tf_op jit(solution)/shard_map/reduce_scatter | solution.py:301
  124.5 2.2 copy-start.2
  160.4 0.7 copy-start.7
  160.4 1.0 copy-start.9
  160.4 1.2 copy-start.8
  160.4 103.5 %copy-start.4 = (bf16[2048,128]{1,0:T(8,128)(2,1)S(1)}, bf16[2048,128]{1,0:T(8,128)(2,1)}, u32[]{:S(2)}) copy-start(bf16[2048,128]{1,0:T(8,128)(2,1)} %w_proj.1) | copy-start | bytes 1572868
  263.9 1.0 copy-start.5
Sparse Core Ops, SparseCore 0:
  43.3 81.2 all-gather.1
  160.5 103.2 reduce-scatter.1

commit v2 on v1

--- a/solution.py
+++ b/solution.py
@@ -62,41 +62,70 @@
         mixed[:, lanes] = jnp.dot(probs, values, preferred_element_type=f32).astype(bf16)
 
 
-def partner_barrier(other):
+def partner_barrier(peers):
     barrier = pltpu.get_barrier_semaphore()
-    pl.semaphore_signal(
-        barrier, inc=1, device_id={"narrow": other}, device_id_type=pl.DeviceIdType.MESH
-    )
-    pl.semaphore_wait(barrier, 1)
+    me = lax.axis_index("narrow")
+    for k in range(1, peers):
+        pl.semaphore_signal(
+            barrier,
+            inc=1,
+            device_id={"narrow": (me + k) % peers},
+            device_id_type=pl.DeviceIdType.MESH,
+        )
+    pl.semaphore_wait(barrier, peers - 1)
+
+
+def send_peers(peers, src, slot, send_sem, recv_sem, piece):
+    me = lax.axis_index("narrow")
+    copies = []
+    for k in range(1, peers):
+        copy = pltpu.make_async_remote_copy(
+            src_ref=src,
+            dst_ref=slot(k),
+            send_sem=send_sem.at[k, piece],
+            recv_sem=recv_sem.at[k, piece],
+            device_id={"narrow": (me + k) % peers},
+            device_id_type=pl.DeviceIdType.MESH,
+        )
+        copy.start()
+        copies.append(copy)
+    return copies
+
+
+def sum_peers(peers, load):
+    me = lax.axis_index("narrow")
+    return sum(load((me - j + peers) % peers).astype(f32) for j in range(peers))
 
 
 def join_kernel(
-    pieces, experts, mixed, w_out, tokens, gain, w_router, routes,
-    hidden, extended, mine, theirs, send_sem, recv_sem,
+    peers, pieces, experts, mixed, w_out, tokens, gain, w_router, routes,
+    hidden, extended, parts, send_sem, recv_sem,
 ):
-    other = 1 - lax.axis_index("narrow")
-    partner_barrier(other)
+    partner_barrier(peers)
     width = w_out.shape[1]
     step = width // pieces
     copies = []
     for piece in range(pieces):
         lanes = pl.ds(piece * step, step)
-        mine[piece] = jnp.dot(mixed[...], w_out[:, lanes], preferred_element_type=f32).astype(bf16)
-        copy = pltpu.make_async_remote_copy(
-            src_ref=mine.at[piece],
-            dst_ref=theirs.at[piece],
-            send_sem=send_sem.at[piece],
-            recv_sem=recv_sem.at[piece],
-            device_id={"narrow": other},
-            device_id_type=pl.DeviceIdType.MESH,
-        )
-        copy.start()
-        copies.append(copy)
+        parts[0, piece] = jnp.dot(
+            mixed[...], w_out[:, lanes], preferred_element_type=f32
+        ).astype(bf16)
+        copies.append(
+            send_peers(
+                peers,
+                parts.at[0, piece],
+                lambda k: parts.at[k, piece],
+                send_sem,
+                recv_sem,
+                piece,
+            )
+        )
     total = 0.0
     for piece in range(pieces):
         lanes = pl.ds(piece * step, step)
-        copies[piece].wait()
-        attn = mine[piece].astype(f32) + theirs[piece].astype(f32)
+        for copy in copies[piece]:
+            copy.wait()
+        attn = sum_peers(peers, lambda k: parts[k, piece])
         row = (tokens[:, lanes].astype(f32) + attn).astype(bf16)
         hidden[:, lanes] = row
         row = row.astype(f32)
@@ -117,6 +146,151 @@
     extended[:, width:] = jnp.where(first, high, gates - high).astype(bf16)
 
 
+def gather_kernel(depth, own, out, local_sem, z_sem, x_sem, y_sem, dx_sem, dy_sem, core_sem):
+    wide, narrow = lax.axis_index("wide"), lax.axis_index("narrow")
+    z, side, core = wide // 4, wide // 2 % 2, wide % 2
+    share = own.shape[0]
+    half = share // 2
+    to_up, to_down = {"wide": wide + 4}, {"wide": wide - 4}
+    to_x, to_y = {"wide": wide + 2 - 4 * side}, {"narrow": 1 - narrow}
+    to_core = {"wide": wide + 1 - 2 * core}
+
+    barrier = pltpu.get_barrier_semaphore()
+
+    def greet(device):
+        pl.semaphore_signal(
+            barrier, inc=1, device_id=device, device_id_type=pl.DeviceIdType.MESH
+        )
+
+    for device in (to_x, to_y, to_core):
+        greet(device)
+    pl.when(z < depth - 1)(lambda: greet(to_up))
+    pl.when(z > 0)(lambda: greet(to_down))
+    pl.semaphore_wait(barrier, 3 + (z + depth - 1) // depth + (2 * depth - 2 - z) // depth)
+
+    def place(s, across_x, across_y, part=None, cores=core):
+        along = 1 - side if across_x else side
+        lane = 1 - narrow if across_y else narrow
+        at = ((s * 4 + along * 2 + cores) * 2 + lane) * share
+        if part is None:
+            return out.at[pl.ds(pl.multiple_of(at, 16), share)]
+        return out.at[pl.ds(pl.multiple_of(at + part * half, 16), half)]
+
+    def copy(ref, sems, index, device):
+        return pltpu.make_async_remote_copy(
+            src_ref=ref,
+            dst_ref=ref,
+            send_sem=sems.at[0, index],
+            recv_sem=sems.at[1, index],
+            device_id=device,
+            device_id_type=pl.DeviceIdType.MESH,
+        )
+
+    def upward(s):
+        return copy(place(s, 0, 0), z_sem, s, to_up)
+
+    def downward(s):
+        return copy(place(s, 0, 0), z_sem, s + depth, to_down)
+
+    def cross(s, kind):
+        return copy(place(s, kind & 1, kind >> 1), core_sem, s * 4 + kind, to_core)
+
+    def over_x(s):
+        return copy(place(s, 0, 0), x_sem, s, to_x)
+
+    def over_y(s):
+        return copy(place(s, 0, 0), y_sem, s, to_y)
+
+    def corner_y(s):
+        return copy(place(s, 1, 0, 0), dy_sem, s, to_y)
+
+    def corner_x(s):
+        return copy(place(s, 0, 1, 1), dx_sem, s, to_x)
+
+    def first(s, up, down):
+        if up:
+            pl.when(z < depth - 1)(lambda: upward(s).start())
+        if down:
+            pl.when(z > 0)(lambda: downward(s).start())
+        over_x(s).start()
+        over_y(s).start()
+        cross(s, 0).start()
+
+    def second(s):
+        over_x(s).wait_recv()
+        corner_y(s).start()
+        cross(s, 1).start()
+        over_y(s).wait_recv()
+        corner_x(s).start()
+        cross(s, 2).start()
+
+    def third(s):
+        corner_y(s).wait_recv()
+        corner_x(s).wait_recv()
+        cross(s, 3).start()
+
+    def at_distance(d, do):
+        if d == 0:
+            do(z, True, True)
+            return
+        pl.when(z >= d)(lambda: do(z - d, True, False))
+        pl.when(z + d < depth)(lambda: do(z + d, False, True))
+
+    def begin(s, up, down):
+        if not (up and down):
+            (upward(s) if up else downward(s)).wait_recv()
+        first(s, up, down)
+
+    keep = pltpu.make_async_copy(own, place(z, 0, 0), local_sem)
+    keep.start()
+    keep.wait()
+    for d in range(depth + 2):
+        if d < depth:
+            at_distance(d, begin)
+        if 0 <= d - 1 < depth:
+            at_distance(d - 1, lambda s, up, down: second(s))
+        if 0 <= d - 2:
+            at_distance(d - 2, lambda s, up, down: third(s))
+
+    def finish(s, up, down):
+        if up:
+            pl.when(z < depth - 1)(lambda: upward(s).wait_send())
+        if down:
+            pl.when(z > 0)(lambda: downward(s).wait_send())
+        for done in (over_x(s), over_y(s), corner_x(s), corner_y(s)):
+            done.wait_send()
+        for kind in range(4):
+            cross(s, kind).wait()
+
+    for d in range(depth):
+        at_distance(d, finish)
+
+
+def gather(own, identity, name):
+    if lax.axis_size("narrow") != 2 or lax.axis_size("wide") % 4:
+        return lax.all_gather(own, ("wide", "narrow"), axis=0, tiled=True)
+    devices = lax.axis_size("wide") * lax.axis_size("narrow")
+    depth = lax.axis_size("wide") // 4
+    pair = pltpu.SemaphoreType.DMA((2, depth))
+    return pl.pallas_call(
+        functools.partial(gather_kernel, depth),
+        out_shape=jax.ShapeDtypeStruct((devices * own.shape[0], own.shape[1]), own.dtype),
+        in_specs=[pl.BlockSpec(memory_space=pl.ANY)],
+        out_specs=pl.BlockSpec(memory_space=pl.ANY),
+        scratch_shapes=[
+            pltpu.SemaphoreType.DMA,
+            pltpu.SemaphoreType.DMA((2, 2 * depth)),
+            pair,
+            pair,
+            pair,
+            pair,
+            pltpu.SemaphoreType.DMA((2, 4 * depth)),
+        ],
+        compiler_params=pltpu.CompilerParams(collective_id=identity, has_side_effects=True),
+        name=name,
+    )(own)
+
+
 def moe_kernel(rows, chosen, w_gate, w_up, w_down, out):
     width = out.shape[1]
     x = rows[:, :width]
@@ -132,29 +306,30 @@
 
 
 def tail_kernel(
-    pieces, partial_out, hidden, gain, w_proj, layer_out, vectors, theirs, send_sem, recv_sem
+    peers, pieces, partial_out, hidden, gain, w_proj,
+    layer_out, vectors, theirs, send_sem, recv_sem,
 ):
-    other = 1 - lax.axis_index("narrow")
-    partner_barrier(other)
-    width = hidden.shape[1]
+    partner_barrier(peers)
     step = hidden.shape[0] // pieces
     copies = []
     for piece in range(pieces):
         rows = pl.ds(piece * step, step)
-        copy = pltpu.make_async_remote_copy(
-            src_ref=partial_out.at[rows],
-            dst_ref=theirs.at[rows],
-            send_sem=send_sem.at[piece],
-            recv_sem=recv_sem.at[piece],
-            device_id={"narrow": other},
-            device_id_type=pl.DeviceIdType.MESH,
-        )
-        copy.start()
-        copies.append(copy)
+        copies.append(
+            send_peers(
+                peers,
+                partial_out.at[rows],
+                lambda k: theirs.at[k, rows],
+                send_sem,
+                recv_sem,
+                piece,
+            )
+        )
+    theirs[0] = partial_out[...]
     for piece in range(pieces):
         rows = pl.ds(piece * step, step)
-        copies[piece].wait()
-        moe = partial_out[rows, :].astype(f32) + theirs[rows, :].astype(f32)
+        for copy in copies[piece]:
+            copy.wait()
+        moe = sum_peers(peers, lambda k: theirs[k, rows, :])
         out = (hidden[rows, :].astype(f32) + moe).astype(bf16)
         layer_out[rows, :] = out
         normed = rms_norm(out.astype(f32), gain[...]).astype(bf16)
@@ -217,6 +392,7 @@
     shards = request_lengths.shape[0]
     wide = lax.axis_index("wide")
     narrow = lax.axis_index("narrow")
+    peers = lax.axis_size("narrow")
 
     lengths_row = lax.dynamic_slice_in_dim(request_lengths, wide, 1, 0)[0]
     member, offsets = request_layout(lengths_row, count)
@@ -254,7 +430,7 @@
     )
     pieces = 4
     hidden, extended = pl.pallas_call(
-        functools.partial(join_kernel, pieces, experts),
+        functools.partial(join_kernel, peers, pieces, experts),
         out_shape=(
             jax.ShapeDtypeStruct((count, width), bf16),
             jax.ShapeDtypeStruct((count, width + extra), bf16),
@@ -262,10 +438,9 @@
         in_specs=[VMEM] * 6,
         out_specs=(VMEM, VMEM),
         scratch_shapes=[
-            pltpu.VMEM((pieces, count, width // pieces), bf16),
-            pltpu.VMEM((pieces, count, width // pieces), bf16),
-            pltpu.SemaphoreType.DMA((pieces,)),
-            pltpu.SemaphoreType.DMA((pieces,)),
+            pltpu.VMEM((peers, pieces, count, width // pieces), bf16),
+            pltpu.SemaphoreType.DMA((peers, pieces)),
+            pltpu.SemaphoreType.DMA((peers, pieces)),
         ],
         compiler_params=pltpu.CompilerParams(
             collective_id=0, has_side_effects=True, vmem_limit_bytes=24 * MIB
@@ -273,9 +448,9 @@
         name="join",
     )(mixed, w_out, tokens, norm_gains[1:2], routers, routes)
 
-    share = count // lax.axis_size("narrow")
+    share = count // peers
     own_rows = lax.dynamic_slice_in_dim(extended, narrow * share, share, 0)
-    rows = lax.all_gather(own_rows, ("wide", "narrow"), axis=0, tiled=True)
+    rows = gather(own_rows, 2, "gather_rows")
 
     ids = wide * experts_here + jnp.arange(experts_here, dtype=jnp.int32)
     lane = jnp.arange(extra, dtype=jnp.int32)[None, :]
@@ -302,7 +477,7 @@
 
     pieces = 4
     layer_out, vectors = pl.pallas_call(
-        functools.partial(tail_kernel, pieces),
+        functools.partial(tail_kernel, peers, pieces),
         out_shape=(
             jax.ShapeDtypeStruct((count, width), bf16),
             jax.ShapeDtypeStruct((count, w_proj.shape[1]), bf16),
@@ -310,9 +485,9 @@
         in_specs=[VMEM] * 4,
         out_specs=(VMEM, VMEM),
         scratch_shapes=[
-            pltpu.VMEM((count, width), bf16),
-            pltpu.SemaphoreType.DMA((pieces,)),
-            pltpu.SemaphoreType.DMA((pieces,)),
+            pltpu.VMEM((peers, count, width), bf16),
+            pltpu.SemaphoreType.DMA((peers, pieces)),
+            pltpu.SemaphoreType.DMA((peers, pieces)),
         ],
         compiler_params=pltpu.CompilerParams(
             collective_id=1, has_side_effects=True, vmem_limit_bytes=24 * MIB
@@ -320,7 +495,8 @@
         name="tail",
     )(scattered, hidden, norm_gains[2:3], w_proj)
 
-    every_vector = lax.all_gather(vectors, "wide", axis=0, tiled=True)
+    own_vectors = lax.dynamic_slice_in_dim(vectors, narrow * share, share, 0)
+    every_vector = gather(own_vectors, 3, "gather_vectors")
 
     flat_lengths = request_lengths.reshape(-1)
     starts = jnp.cumsum(request_lengths, axis=1) - request_lengths

time: 313 us -> 284 us (0.907)
  waiting for transfers between devices: 183 us -> 102 us
  Pallas kernels: 74 us -> 149 us
  blocking collectives: 23.1 us -> 0 us
    all_gather x1 -> x0, waiting for transfers between devices: 81.2 us -> none  [body(): rows = lax.all_gather(own_rows, ('wide', 'narrow'), axis=0, tiled=True)]
    pallas_call x2 -> x4, Pallas kernels: 30.1 us -> 105 us  [the longest x2 74.6 us: gather(): pl.pallas_call(functools.partial(gather_kernel, depth), out_shape=jax.Sha...]
    all_gather x1 -> x0, blocking collectives: 23.1 us -> none  [body(): every_vector = lax.all_gather(vectors, 'wide', axis=0, tiled=True)]
  transfers between devices with their start and end apart: 2 -> 1, of which waited for: 2 -> 1; matrix products, arithmetic and copies ran while one was open for 0% -> 0% of each run, Pallas kernels for 0% -> 0%
where the time goes in v2:
time: 284 us
  Pallas kernels  149 us (52%)
  waiting for transfers between devices  102 us (36%)
  local copies, waits for them, and re-layouts  16.3 us (6%)
  between operations  14.2 us (5%)
    reduce_scatter x1, waiting for transfers between devices, body(): lax.psum_scatter(partial_out, 'wide', scatter_dimension=0, tiled=True)  102 us
    pallas_call x2, Pallas kernels, gather(): pl.pallas_call(functools.partial(gather_kernel, depth), out_shape=jax.Sha...  74.6 us
    pallas_call x1, Pallas kernels, body(): pl.pallas_call(moe_kernel, out_shape=jax.ShapeDtypeStruct((every, width),...  33.6 us
    pallas_call x1, Pallas kernels, body(): pl.pallas_call(functools.partial(join_kernel, peers, pieces, experts), ou...  16 us
    pallas_call x1, Pallas kernels, body(): pl.pallas_call(functools.partial(tail_kernel, peers, pieces), out_shape=(...  14.3 us
    unnamed x24, local copies, waits for them, and re-layouts  13.7 us
    pallas_call x1, Pallas kernels, body(): pl.pallas_call(front_kernel, out_shape=jax.ShapeDtypeStruct((count, colum...  7.96 us
  transfers between devices with their start and end apart: 1, of which 1 were waited for; matrix products, arithmetic and copies ran while one was open for 0% of the time, Pallas kernels for 0%

profile of v2, /device:TPU:0, one launch (start us, length us, event | category | flops | bytes accessed | tf_op | source)
XLA Modules:
  0.0 283.8 jit_solution(14983996059238034495)
XLA Ops:
  7.2 0.0 reduce-scatter.2.cloned.1.call-start
  7.2 0.8 copy.29
  8.0 0.2 reduce-window.4
  8.2 0.1 fusion.1
  8.3 0.1 compare_convert_fusion.bias
  8.4 0.1 select_reduce_fusion.2
  8.5 0.9 fusion.4
  9.4 0.8 copy.32.routes
  10.2 1.2 copy.30
  11.4 0.1 pad.6.clone
  11.4 0.3 fusion
  11.7 0.3 maximum_maximum_fusion.w_router
  12.1 0.1 pad_maximum_fusion
  12.2 0.0 copy-start
  12.2 4.6 %copy-done = bf16[2048,3,1024]{2,0,1:T(8,128)(2,1)S(1)} copy-done((bf16[2048,3,1024]{2,0,1:T(8,128)(2,1)S(1)}, bf16[2048,3,1024]{2,0,1:T(8,128)(2,1)}, u32[]{:S(2)}) %copy-start) | copy-done | bytes 12582936
  16.8 0.0 copy-start.3
  16.8 1.0 copy-done.3
  17.8 0.0 copy-start.6
  17.8 0.7 copy-done.6
  18.5 8.0 %front.1.mixed = bf16[128,1024]{1,0:T(8,128)(2,1)S(1)} custom-call(bf16[128,2048]{1,0:T(8,128)(2,1)S(1)} %copy-done.3, f32[1,2048]{1,0:T(1,128)S(1)} %get-tuple-element.15.gain, bf16[3,2048,1024]{2,1,0:T(8,128)(2,1)S(1)} %bitcast.17, f32[2,1024]{1,0:T(2,128)S(1)} %copy-done.6, f32[128,128]{1,0:T(8,128)S(1)} %get-tuple-element.20.cosine, ...), custom_call_target="tpu_custom_call" | custom-call | tf_op jit(solution)/shard_map/front/pallas_call | solution.py:408
  26.5 0.0 copy-done.1
  26.5 16.0 %join.1 = (bf16[128,2048]{1,0:T(8,128)(2,1)S(1)}, bf16[128,2176]{1,0:T(8,128)(2,1)S(1)}) custom-call(bf16[128,1024]{1,0:T(8,128)(2,1)S(1)} %front.1.mixed, bf16[1024,2048]{1,0:T(8,128)(2,1)S(1)} %copy-done.1, bf16[128,2048]{1,0:T(8,128)(2,1)S(1)} %copy-done.3, f32[1,2048]{1,0:T(1,128)S(1)} %get-tuple-element.16.gain, ...), custom_call_target="tpu_custom_call" | custom-call | tf_op jit(solution)/shard_map/join/pallas_call | solution.py:432
  42.5 0.7 constant_dynamic-slice_fusion.own
  43.2 53.3 %gather_rows.1.rows = bf16[2048,2176]{1,0:T(8,128)(2,1)} custom-call(bf16[64,2176]{1,0:T(8,128)(2,1)} %constant_dynamic-slice_fusion.own), custom_call_target="tpu_custom_call" | custom-call | tf_op jit(solution)/shard_map/gather_rows/pallas_call | solution.py:275
  96.5 0.1 or_convert_fusion.chosen
  96.6 0.0 copy-start.2
  96.6 2.2 copy-done.2
  98.8 33.6 %experts.1 = bf16[2048,2048]{1,0:T(8,128)(2,1)} custom-call(bf16[2048,2176]{1,0:T(8,128)(2,1)} %gather_rows.1.rows, f32[2,128]{1,0:T(2,128)S(1)} %or_convert_fusion.chosen, bf16[2,2048,512]{2,1,0:T(8,128)(2,1)S(1)} %copy-done.2, bf16[2,2048,512]{2,1,0:T(8,128)(2,1)} %w_up.1, bf16[2,512,2048]{2,1,0:T(8,128)(2,1)} %w_down.1), custom_call_target="tpu_custom_call" | custom-call | tf_op jit(solution)/shard_map/experts/pallas_call | solution.py:460
  132.4 0.0 copy-start.9
  132.4 0.0 copy-start.4
  132.4 0.0 reduce-scatter.2.cloned.1.call-update
  132.4 0.6 copy-done.7
  133.1 0.1 broadcast_in_dim.61
  133.2 0.1 copy.33
  133.3 0.1 broadcast_in_dim.58
  133.4 0.0 copy-done.9
  133.4 0.2 select_reduce_fusion.1
  133.6 0.0 copy-done.8
  133.6 0.1 convert_reduce_fusion.1
  133.7 0.6 pad_add_fusion.plan
  134.3 102.3 %reduce-scatter.2.cloned.1.call-done.partial_out = bf16[128,2048]{1,0:T(8,128)(2,1)} async-done(((bf16[2048,2048]{1,0:T(8,128)(2,1)}), bf16[128,2048]{1,0:T(8,128)(2,1)}) %reduce-scatter.2.cloned.1.call-update) | async-done | bytes 524304 | tf_op jit(solution)/shard_map/reduce_scatter | solution.py:476
  236.6 0.0 copy-done.4
  236.6 1.0 copy-done.5
  237.6 14.3 %tail.1 = (bf16[128,2048]{1,0:T(8,128)(2,1)S(1)}, bf16[128,128]{1,0:T(8,128)(2,1)S(1)}) custom-call(bf16[128,2048]{1,0:T(8,128)(2,1)S(1)} %copy-done.5, bf16[128,2048]{1,0:T(8,128)(2,1)S(1)} %get-tuple-element.7.hidden, f32[1,2048]{1,0:T(1,128)S(1)} %get-tuple-element.14.gain, bf16[2048,128]{1,0:T(8,128)(2,1)S(1)} %copy-done.4), custom_call_target="tpu_custom_call" | custom-call | tf_op jit(solution)/shard_map/tail/pallas_call | solution.py:479
  251.9 0.6 constant_dynamic-slice_fusion.1.own
  252.5 21.3 %gather_vectors.1.vectors = bf16[2048,128]{1,0:T(8,128)(2,1)} custom-call(bf16[64,128]{1,0:T(8,128)(2,1)} %constant_dynamic-slice_fusion.1.own), custom_call_target="tpu_custom_call" | custom-call | tf_op jit(solution)/shard_map/gather_vectors/pallas_call | solution.py:275
  273.9 2.3 docs.2
  276.2 0.8 copy.36
  (14 shorter events, 0.1 us)
Async XLA Ops:
  7.2 229.4 %reduce-scatter.2.cloned.1.call-start = ((), (), s32[]{:S(2)}) async-start(), calls=%async_computation.1 | async-start | bytes 8912896 | tf_op jit(solution)/shard_map/reduce_scatter | solution.py:476
  12.2 4.6 %copy-start = (bf16[2048,3,1024]{2,0,1:T(8,128)(2,1)S(1)}, bf16[2048,3,1024]{2,0,1:T(8,128)(2,1)}, u32[]{:S(2)}) copy-start(bf16[2048,3,1024]{2,0,1:T(8,128)(2,1)} %param.17) | copy-start | bytes 37748740
  16.8 1.0 copy-start.3
  17.8 0.7 copy-start.6
  18.5 8.0 %copy-start.1 = (bf16[1024,2048]{1,0:T(8,128)(2,1)S(1)}, bf16[1024,2048]{1,0:T(8,128)(2,1)}, u32[]{:S(2)}) copy-start(bf16[1024,2048]{1,0:T(8,128)(2,1)} %w_out.1) | copy-start | bytes 12582916
  96.6 2.2 copy-start.2
  132.4 0.7 copy-start.7
  132.4 1.0 copy-start.9
  132.4 1.2 copy-start.8
  132.4 104.2 %copy-start.4 = (bf16[2048,128]{1,0:T(8,128)(2,1)S(1)}, bf16[2048,128]{1,0:T(8,128)(2,1)}, u32[]{:S(2)}) copy-start(bf16[2048,128]{1,0:T(8,128)(2,1)} %w_proj.1) | copy-start | bytes 1572868
  236.6 1.0 copy-start.5
Sparse Core Ops, SparseCore 0:
  132.6 104.0 reduce-scatter.1

commit v3 on v2

--- a/solution.py
+++ b/solution.py
@@ -293,8 +293,9 @@
 
 def moe_kernel(rows, chosen, w_gate, w_up, w_down, out):
     width = out.shape[1]
-    x = rows[:, :width]
-    table = rows[:, width:].astype(f32)
+    block = rows[...].reshape(out.shape[0], rows.shape[2])
+    x = block[:, :width]
+    table = block[:, width:].astype(f32)
     total = 0.0
     for e in range(w_gate.shape[0]):
         gate = jnp.sum(table * chosen[e : e + 1, :], axis=-1, keepdims=True)
@@ -455,25 +456,36 @@
     ids = wide * experts_here + jnp.arange(experts_here, dtype=jnp.int32)
     lane = jnp.arange(extra, dtype=jnp.int32)[None, :]
     chosen = ((lane == ids[:, None]) | (lane == ids[:, None] + experts)).astype(f32)
-    every = rows.shape[0]
-    block = 256
-    partial_out = pl.pallas_call(
-        moe_kernel,
-        out_shape=jax.ShapeDtypeStruct((every, width), bf16),
-        grid=(every // block,),
-        in_specs=[
-            pl.BlockSpec((block, width + extra), lambda i: (i, 0)),
-            pl.BlockSpec(chosen.shape, lambda i: (0, 0)),
-            pl.BlockSpec(w_gate.shape, lambda i: (0, 0, 0)),
-            pl.BlockSpec(w_up.shape, lambda i: (0, 0, 0)),
-            pl.BlockSpec(w_down.shape, lambda i: (0, 0, 0)),
-        ],
-        out_specs=pl.BlockSpec((block, width), lambda i: (i, 0)),
-        compiler_params=pltpu.CompilerParams(vmem_limit_bytes=48 * MIB),
-        name="experts",
-    )(rows, chosen, w_gate, w_up, w_down)
-
-    scattered = lax.psum_scatter(partial_out, "wide", scatter_dimension=0, tiled=True)
+    halves = 2
+    depth = count // halves
+    view = rows.reshape(shards, halves, depth, width + extra)
+    group = 4
+    scattered = []
+    for part in range(halves):
+        partial_out = pl.pallas_call(
+            moe_kernel,
+            out_shape=jax.ShapeDtypeStruct((shards * depth, width), bf16),
+            grid=(shards // group,),
+            in_specs=[
+                pl.BlockSpec(
+                    (group, None, depth, width + extra), lambda i, part=part: (i, part, 0, 0)
+                ),
+                pl.BlockSpec(chosen.shape, lambda i: (0, 0)),
+                pl.BlockSpec(w_gate.shape, lambda i: (0, 0, 0)),
+                pl.BlockSpec(w_up.shape, lambda i: (0, 0, 0)),
+                pl.BlockSpec(w_down.shape, lambda i: (0, 0, 0)),
+            ],
+            out_specs=pl.BlockSpec((group * depth, width), lambda i: (i, 0)),
+            compiler_params=pltpu.CompilerParams(vmem_limit_bytes=48 * MIB),
+            cost_estimate=pl.CostEstimate(
+                flops=6 * shards * depth * w_gate.size,
+                bytes_accessed=6 * w_gate.size + 4 * shards * depth * width,
+                transcendentals=0,
+            ),
+            name="experts",
+        )(view, chosen, w_gate, w_up, w_down)
+        scattered.append(lax.psum_scatter(partial_out, "wide", scatter_dimension=0, tiled=True))
+    scattered = jnp.concatenate(scattered, axis=0)
 
     pieces = 4
     layer_out, vectors = pl.pallas_call(

time: 284 us -> 311 us (1.095)
  waiting for transfers between devices: 102 us -> 125 us
    reduce_scatter x1 -> x2, waiting for transfers between devices: 102 us -> 125 us  [body(): lax.psum_scatter(partial_out, 'wide', scatter_dimension=0, tiled=True)]
    pallas_call x1 -> x2, Pallas kernels: 33.6 us -> 38.4 us  [body(): pl.pallas_call(moe_kernel, out_shape=jax.ShapeDtypeStruct((shards * depth...]
  transfers between devices with their start and end apart: 1 -> 2, of which waited for: 1 -> 2; matrix products, arithmetic and copies ran while one was open for 0% -> 0% of each run, Pallas kernels for 0% -> 6%
where the time goes in v3:
time: 311 us
  Pallas kernels  151 us (49%)
  waiting for transfers between devices  125 us (40%)
  local copies, waits for them, and re-layouts  16.9 us (5%)
  between operations  14.2 us (5%)
  other arithmetic  3.3 us (1%)
    reduce_scatter x2, waiting for transfers between devices, body(): lax.psum_scatter(partial_out, 'wide', scatter_dimension=0, tiled=True)  125 us
    pallas_call x2, Pallas kernels, gather(): pl.pallas_call(functools.partial(gather_kernel, depth), out_shape=jax.Sha...  74 us
    pallas_call x2, Pallas kernels, body(): pl.pallas_call(moe_kernel, out_shape=jax.ShapeDtypeStruct((shards * depth...  38.4 us
    pallas_call x1, Pallas kernels, body(): pl.pallas_call(functools.partial(join_kernel, peers, pieces, experts), ou...  16 us
    unnamed x24, local copies, waits for them, and re-layouts  14.3 us
    pallas_call x1, Pallas kernels, body(): pl.pallas_call(functools.partial(tail_kernel, peers, pieces), out_shape=(...  12.6 us
    pallas_call x1, Pallas kernels, body(): pl.pallas_call(front_kernel, out_shape=jax.ShapeDtypeStruct((count, colum...  7.96 us
  transfers between devices with their start and end apart: 2, of which 2 were waited for; matrix products, arithmetic and copies ran while one was open for 0% of the time, Pallas kernels for 6%

profile of v3, /device:TPU:0, one launch (start us, length us, event | category | flops | bytes accessed | tf_op | source)
XLA Modules:
  0.0 310.7 jit_solution(16977851197716888985)
XLA Ops:
  7.2 0.0 reduce-scatter.3.cloned.1.call-start
  7.2 0.8 copy.29
  8.0 0.2 reduce-window.4
  8.2 0.1 fusion.1
  8.3 0.1 compare_convert_fusion.bias
  8.4 0.1 select_reduce_fusion.2
  8.5 0.9 fusion.4
  9.4 1.2 copy.30
  10.5 0.8 copy.32.routes
  11.3 0.3 fusion
  11.7 0.1 pad.8.clone
  11.7 0.3 maximum_maximum_fusion.w_router
  12.1 0.1 pad_maximum_fusion.1
  12.2 0.0 copy-start
  12.2 4.6 %copy-done = bf16[2048,3,1024]{2,0,1:T(8,128)(2,1)S(1)} copy-done((bf16[2048,3,1024]{2,0,1:T(8,128)(2,1)S(1)}, bf16[2048,3,1024]{2,0,1:T(8,128)(2,1)}, u32[]{:S(2)}) %copy-start) | copy-done | bytes 12582936
  16.8 1.0 copy-done.4
  17.8 0.7 copy-done.6
  18.5 8.0 %front.1.mixed = bf16[128,1024]{1,0:T(8,128)(2,1)S(1)} custom-call(bf16[128,2048]{1,0:T(8,128)(2,1)S(1)} %copy-done.4, f32[1,2048]{1,0:T(1,128)S(1)} %get-tuple-element.15.gain, bf16[3,2048,1024]{2,1,0:T(8,128)(2,1)S(1)} %bitcast.18, f32[2,1024]{1,0:T(2,128)S(1)} %copy-done.6, f32[128,128]{1,0:T(8,128)S(1)} %get-tuple-element.20.cosine, ...), custom_call_target="tpu_custom_call" | custom-call | tf_op jit(solution)/shard_map/front/pallas_call | solution.py:409
  26.5 0.0 copy-done.1
  26.5 16.0 %join.1 = (bf16[128,2048]{1,0:T(8,128)(2,1)S(1)}, bf16[128,2176]{1,0:T(8,128)(2,1)S(1)}) custom-call(bf16[128,1024]{1,0:T(8,128)(2,1)S(1)} %front.1.mixed, bf16[1024,2048]{1,0:T(8,128)(2,1)S(1)} %copy-done.1, bf16[128,2048]{1,0:T(8,128)(2,1)S(1)} %copy-done.4, f32[1,2048]{1,0:T(1,128)S(1)} %get-tuple-element.16.gain, ...), custom_call_target="tpu_custom_call" | custom-call | tf_op jit(solution)/shard_map/join/pallas_call | solution.py:433
  42.5 0.7 constant_dynamic-slice_fusion.own
  43.2 53.3 %gather_rows.1 = bf16[2048,2176]{1,0:T(8,128)(2,1)} custom-call(bf16[64,2176]{1,0:T(8,128)(2,1)} %constant_dynamic-slice_fusion.own), custom_call_target="tpu_custom_call" | custom-call | tf_op jit(solution)/shard_map/gather_rows/pallas_call | solution.py:275
  96.5 0.1 or_convert_fusion.chosen
  96.6 19.1 %experts.2 = bf16[1024,2048]{1,0:T(8,128)(2,1)S(1)} custom-call(bf16[16,2,64,2176]{3,2,1,0:T(8,128)(2,1)} %bitcast.19, f32[2,128]{1,0:T(2,128)S(1)} %or_convert_fusion.chosen, bf16[2,2048,512]{2,1,0:T(8,128)(2,1)} %w_gate.3, bf16[2,2048,512]{2,1,0:T(8,128)(2,1)} %w_up.3, bf16[2,512,2048]{2,1,0:T(8,128)(2,1)} %w_down.3), custom_call_target="tpu_custom_call" | custom-call | flops 12884901888 | bytes 20971520 | tf_op jit(solution)/shard_map/experts/pallas_call | solution.py:465
  115.7 0.0 copy-start.2
  115.7 2.0 copy-done.2
  117.7 0.0 reduce-scatter.3.cloned.1.call-update
  117.7 0.2 reduce-scatter.5.cloned.1.call-start
  117.9 19.3 %experts.3 = bf16[1024,2048]{1,0:T(8,128)(2,1)S(1)} custom-call(bf16[16,2,64,2176]{3,2,1,0:T(8,128)(2,1)} %bitcast.20, f32[2,128]{1,0:T(2,128)S(1)} %or_convert_fusion.chosen, bf16[2,2048,512]{2,1,0:T(8,128)(2,1)} %w_gate.3, bf16[2,2048,512]{2,1,0:T(8,128)(2,1)} %w_up.3, bf16[2,512,2048]{2,1,0:T(8,128)(2,1)} %w_down.3), custom_call_target="tpu_custom_call" | custom-call | flops 12884901888 | bytes 20971520 | tf_op jit(solution)/shard_map/experts/pallas_call | solution.py:465
  137.2 0.0 copy-start.3
  137.2 1.9 copy-done.3
  139.2 0.0 reduce-scatter.5.cloned.1.call-update
  139.2 0.1 broadcast_in_dim.61
  139.3 0.6 copy-done.7
  139.9 0.1 copy.33
  140.0 0.1 broadcast_in_dim.58
  140.1 0.0 copy-done.9
  140.1 0.2 select_reduce_fusion.1
  140.3 0.1 convert_reduce_fusion.1
  140.4 0.6 pad_add_fusion.plan
  141.0 48.9 %reduce-scatter.3.cloned.1.call-done = bf16[64,2048]{1,0:T(8,128)(2,1)} async-done(((bf16[1024,2048]{1,0:T(8,128)(2,1)}), bf16[64,2048]{1,0:T(8,128)(2,1)}) %reduce-scatter.3.cloned.1.call-update) | async-done | bytes 262160 | tf_op jit(solution)/shard_map/reduce_scatter | solution.py:487
  189.9 75.8 %reduce-scatter.5.cloned.1.call-done = bf16[64,2048]{1,0:T(8,128)(2,1)} async-done(((bf16[1024,2048]{1,0:T(8,128)(2,1)}), bf16[64,2048]{1,0:T(8,128)(2,1)}) %reduce-scatter.5.cloned.1.call-update) | async-done | bytes 262160 | tf_op jit(solution)/shard_map/reduce_scatter | solution.py:487
  265.7 1.1 pad_maximum_fusion.partial_out
  266.8 12.6 %tail.1 = (bf16[128,2048]{1,0:T(8,128)(2,1)S(1)}, bf16[128,128]{1,0:T(8,128)(2,1)S(1)}) custom-call(bf16[128,2048]{1,0:T(8,128)(2,1)S(1)} %pad_maximum_fusion.partial_out, bf16[128,2048]{1,0:T(8,128)(2,1)S(1)} %get-tuple-element.7.hidden, f32[1,2048]{1,0:T(1,128)S(1)} %get-tuple-element.14.gain, bf16[2048,128]{1,0:T(8,128)(2,1)S(1)} %copy-done.5), custom_call_target="tpu_custom_call" | custom-call | tf_op jit(solution)/shard_map/tail/pallas_call | solution.py:491
  279.4 0.6 constant_dynamic-slice_fusion.1.own
  280.0 20.7 %gather_vectors.1.vectors = bf16[2048,128]{1,0:T(8,128)(2,1)} custom-call(bf16[64,128]{1,0:T(8,128)(2,1)} %constant_dynamic-slice_fusion.1.own), custom_call_target="tpu_custom_call" | custom-call | tf_op jit(solution)/shard_map/gather_vectors/pallas_call | solution.py:275
  300.7 2.3 docs.2
  303.0 0.8 copy.36
  (19 shorter events, 0.1 us)
Async XLA Ops:
  7.2 182.8 %reduce-scatter.3.cloned.1.call-start = ((), (), s32[]{:S(2)}) async-start(), calls=%async_computation.2 | async-start | bytes 4456448 | tf_op jit(solution)/shard_map/reduce_scatter | solution.py:487
  12.2 4.6 %copy-start = (bf16[2048,3,1024]{2,0,1:T(8,128)(2,1)S(1)}, bf16[2048,3,1024]{2,0,1:T(8,128)(2,1)}, u32[]{:S(2)}) copy-start(bf16[2048,3,1024]{2,0,1:T(8,128)(2,1)} %param.17) | copy-start | bytes 37748740
  16.8 1.0 copy-start.4
  17.8 0.7 copy-start.6
  18.5 8.0 %copy-start.1 = (bf16[1024,2048]{1,0:T(8,128)(2,1)S(1)}, bf16[1024,2048]{1,0:T(8,128)(2,1)}, u32[]{:S(2)}) copy-start(bf16[1024,2048]{1,0:T(8,128)(2,1)} %w_out.1) | copy-start | bytes 12582916
  115.7 2.0 copy-start.2
  117.7 148.0 %reduce-scatter.5.cloned.1.call-start = ((), (), s32[]{:S(2)}) async-start(), calls=%async_computation.3 | async-start | bytes 4456448 | tf_op jit(solution)/shard_map/reduce_scatter | solution.py:487
  137.2 1.9 copy-start.3
  139.2 0.7 copy-start.7
  139.2 0.9 copy-start.9
  139.2 1.1 copy-start.8
  139.2 127.6 %copy-start.5 = (bf16[2048,128]{1,0:T(8,128)(2,1)S(1)}, bf16[2048,128]{1,0:T(8,128)(2,1)}, u32[]{:S(2)}) copy-start(bf16[2048,128]{1,0:T(8,128)(2,1)} %w_proj.1) | copy-start | bytes 1572868
Sparse Core Ops, SparseCore 0:
  117.8 72.0 reduce-scatter.2
  194.3 71.3 reduce-scatter.4
